TPU v7x, 256 devices: a whole 4x4x8 slice. The times are simulated.
256 devices in a mesh: chan: 32 (over x, y, z_lo), tm: 8 (over z_hi, core).
Axes of the slice: x: 4, y: 4, z: 8 (z_hi: 4, z_lo: 2; z = z_hi * 2 + z_lo), core: 2. Of those that a mesh axis runs over, the one named last changes fastest.
Arguments:
- voltages: bfloat16 [2, 2048, 256, 1024], P(None, 'chan', None, 'tm'), may hold values from -7 to 7, as said below
- channel_gains: float32 [2, 2048, 256], P(None, 'chan'), may hold values from -1.5 to 1.5
- weights: bfloat16 [2, 256, 256, 2048], P(None, 'chan', None, 'tm'), may hold values from -0.09375 to 0.09375
- scales: float32 [256], P('chan'), may hold values from 0.5 to 2
- fir_taps: int32 [4, 16], replicated, may hold values from 1 to 16
Outputs:
- formed_beams: float32 [2, 256, 64, 16, 256], P(None, 'chan', 'tm')
Inputs may be any that keep to these rules, and one draw needn't show every extreme that they name: voltages hold whole numbers.
All inputs are finite; a program needn't handle non-finite values.
Results may differ from a plain program's by a relative error of at most 0.0041.
Values may be sent and summed in bfloat16 or wider, within the bound.
A program may use at most 192 MiB of HBM per device.

v0:
```python
import math

import jax
import jax.numpy as jnp
from jax import lax
from jax.sharding import PartitionSpec as P


def from_behind(x, axis, by):
    peers = lax.axis_size(axis)
    pairs = [(i, i + by) for i in range(peers) if 0 <= i + by < peers]
    return lax.ppermute(x, axis, pairs)


def block_tables(length, block):
    positions = jnp.arange(block, dtype=jnp.int32)
    phase = positions % length
    product = phase[:, None] * phase[None, :] % length
    phase_angle = product.astype(jnp.float32) * (2.0 * math.pi / length)
    same_frame = positions[:, None] // length == positions[None, :] // length
    return (
        jnp.where(same_frame, jnp.cos(phase_angle), 0.0),
        jnp.where(same_frame, jnp.sin(phase_angle), 0.0),
    )


def calibrate(voltage, gain_col):
    volt_re = voltage[0].astype(jnp.float32)
    volt_im = voltage[1].astype(jnp.float32)
    gain_re = gain_col[0][..., None]
    gain_im = gain_col[1][..., None]
    return jnp.stack(
        [gain_re * volt_re - gain_im * volt_im, gain_re * volt_im + gain_im * volt_re]
    ).astype(jnp.bfloat16)


def channelize(extended, fir_taps):
    tap_count, length = fir_taps.shape
    halo_len = (tap_count - 1) * length
    span = extended.shape[-1] - halo_len
    tap_coef = fir_taps.astype(jnp.float32) / 16.0
    filtered = jnp.tile(tap_coef[0], span // length) * extended[
        ..., halo_len : halo_len + span
    ].astype(jnp.float32)
    for tap_index in range(1, tap_count):
        begin_at = halo_len - length * tap_index
        filtered = filtered + jnp.tile(tap_coef[tap_index], span // length) * extended[
            ..., begin_at : begin_at + span
        ].astype(jnp.float32)
    block = math.gcd(span, 128)
    leading = filtered.shape[1:-1]
    filtered = filtered.reshape((2,) + leading + (span // block, block))
    cosine_table, sine_table = block_tables(length, block)
    dft_norm = 1.0 / math.sqrt(length)
    highest = lax.Precision.HIGHEST
    real_part = (
        jnp.einsum("...k,gk->...g", filtered[0], cosine_table, precision=highest)
        + jnp.einsum("...k,gk->...g", filtered[1], sine_table, precision=highest)
    ) * dft_norm
    imag_part = (
        jnp.einsum("...k,gk->...g", filtered[1], cosine_table, precision=highest)
        - jnp.einsum("...k,gk->...g", filtered[0], sine_table, precision=highest)
    ) * dft_norm
    stacked = jnp.stack([real_part, imag_part]).astype(jnp.bfloat16)
    return stacked.reshape((2,) + leading + (span,))


def arrange(spectra):
    return jnp.transpose(spectra, (2, 3, 0, 1))


def beam_terms(spectra, weight):
    weight_re = weight[0]
    weight_im = weight[1]
    row_re = jnp.stack([weight_re, -weight_im], axis=2)
    row_im = jnp.stack([weight_im, weight_re], axis=2)
    panel_all = jnp.concatenate([row_re, row_im], axis=1)
    return jnp.einsum("cnpx,cypx->cny", spectra, panel_all, preferred_element_type=jnp.float32)


def local_spectra(turned, prior_rim, fir_taps):
    return arrange(channelize(jnp.concatenate([prior_rim, turned], axis=-1), fir_taps))


def shards(voltages, channel_gains, weights, scales, fir_taps):
    tap_count, length = fir_taps.shape
    halo_len = (tap_count - 1) * length
    calibrated = calibrate(voltages, channel_gains)
    local_chans = weights.shape[1]
    beam_count = weights.shape[2]
    turned = lax.all_to_all(calibrated, "chan", split_axis=2, concat_axis=1, tiled=True)
    prior_rim = from_behind(turned[..., turned.shape[-1] - halo_len :], "tm", 1)
    spectra = local_spectra(turned, prior_rim, fir_taps)
    formed = beam_terms(spectra, lax.all_gather(weights, "tm", axis=3, tiled=True))
    formed = formed * scales[:, None, None]
    frames = formed.shape[1] // length
    return jnp.transpose(
        formed.reshape(local_chans, frames, length, 2, beam_count), (3, 0, 1, 2, 4)
    )


def solution(mesh):
    in_specs = (
        P(None, "chan", None, "tm"),
        P(None, "chan", None),
        P(None, "chan", None, "tm"),
        P("chan"),
        P(),
    )
    out_specs = P(None, "chan", "tm", None, None)
    return jax.shard_map(shards, mesh=mesh, in_specs=in_specs, out_specs=out_specs, check_vma=False)
```

profile of v0, /device:TPU:170, one launch (start us, length us, event | category | flops | bytes accessed | tf_op | source)
XLA Modules:
  0.0 483.0 jit_solution(11934870494420804966)
XLA Ops:
  6.5 0.0 all-gather.2.cloned.1.call-start
  6.5 0.7 all-gather.2.cloned.1.call-update
  7.3 0.9 slice_bitcast_fusion.13
  8.1 0.1 copy.11
  8.2 0.1 copy.9
  8.3 4.0 fusion.65
  12.3 18.7 %fusion.3 = (bf16[1,64,256,128]{3,1,0,2:T(8,128)(2,1)S(1)}, bf16[1,64,256,128]{3,1,0,2:T(8,128)(2,1)}) fusion(f32[64,256]{0,1:T(8,128)S(1)} %copy.11, f32[64,256]{0,1:T(8,128)S(1)} %copy.9, bf16[1,64,256,128]{3,2,1,0:T(8,128)(2,1)S(1)} %get-tuple-element.10, bf16[1,64,256,128]{3,2,1,0:T(8,128)(2,1)S(1)} %get-tuple-element.9), kind=kLoop, calls=%fused_computation.13 | loop fusion | flops 20971520 | bytes 16908288 | tf_op jit(solution)/shard_map/convert.4
  31.0 6.4 %pad_maximum_fusion.1 = bf16[2,64,256,128]{3,1,0,2:T(8,128)(2,1)} fusion(bf16[1,64,256,128]{3,1,0,2:T(8,128)(2,1)} %get-tuple-element.8, bf16[1,64,256,128]{3,1,0,2:T(8,128)(2,1)S(1)} %get-tuple-element.7), kind=kLoop, calls=%fused_computation.23 | loop fusion | flops 4194304 | bytes 16777216 | tf_op jit(solution)/shard_map/stack | solution.py:32
  37.4 216.6 %all_to_all.18 = bf16[2,64,256,128]{3,1,0,2:T(8,128)(2,1)} all-to-all(bf16[2,64,256,128]{3,1,0,2:T(8,128)(2,1)} %pad_maximum_fusion.1), channel_id=1, replica_groups=mesh['chan'=32,'tm'=8] {'chan'}, dimensions={2} | all-to-all | bytes 16777216 | tf_op jit(solution)/shard_map/all_to_all | solution.py:91
  254.1 9.6 %copy.13 = bf16[2,64,32,8,128]{4,1,2,3,0:T(8,128)(2,1)} copy(bf16[2,64,32,8,128]{4,1,0,3,2:T(8,128)(2,1)} %bitcast.58) | data formatting | bytes 16777216 | tf_op jit(solution)/shard_map/all_to_all | solution.py:91
  263.6 8.9 %slice.68 = bf16[2,2048,8,48]{3,1,2,0:T(8,128)(2,1)} slice(bf16[2,2048,8,128]{3,1,2,0:T(8,128)(2,1)} %bitcast.56), slice={[0:2], [0:2048], [0:8], [80:128]} | slice | bytes 6291456 | tf_op jit(solution)/shard_map/slice | solution.py:92
  272.5 6.8 %copy.14 = bf16[2,2048,8,48]{1,3,2,0:T(8,128)(2,1)S(1)} copy(bf16[2,2048,8,48]{3,1,2,0:T(8,128)(2,1)} %slice.68) | data formatting | bytes 6291456 | tf_op jit(solution)/shard_map/slice | solution.py:92
  279.3 2.2 collective-permute-start
  281.5 0.0 copy-done.1
  281.6 0.1 mul.135
  281.6 0.1 mul.146
  281.7 0.1 mul.149
  281.8 0.1 mul.152
  281.9 71.9 %collective-permute-done = bf16[2,2048,8,48]{1,3,2,0:T(8,128)(2,1)} collective-permute-done((bf16[2,2048,8,48]{1,3,2,0:T(8,128)(2,1)S(1)}, bf16[2,2048,8,48]{1,3,2,0:T(8,128)(2,1)}, u32[]{:S(2)}, u32[]{:S(2)}) %collective-permute-start) | collective-permute-done | bytes 3145760 | tf_op jit(solution)/shard_map/ppermute | solution.py:12
  353.8 8.3 %copy.15 = bf16[2,2048,8,48]{3,1,2,0:T(8,128)(2,1)} copy(bf16[2,2048,8,48]{1,3,2,0:T(8,128)(2,1)} %collective-permute-done) | data formatting | bytes 6291456 | tf_op jit(solution)/shard_map/ppermute | solution.py:12
  362.1 32.0 %multiply_add_fusion = f32[2,2048,8,128]{3,1,2,0:T(8,128)S(1)} fusion(bf16[2,2048,8,128]{3,1,2,0:T(8,128)(2,1)} %bitcast.57, bf16[2,2048,8,48]{3,1,2,0:T(8,128)(2,1)} %copy.15, f32[128]{0:T(128)S(1)} %mul.152, f32[128]{0:T(128)S(1)} %mul.149, f32[128]{0:T(128)S(1)} %mul.146, f32[128]{0:T(128)S(1)} %mul.135), kind=kLoop, calls=%fused_computation.7 | loop fusion | flops 83886080 | bytes 28313600 | tf_op jit(solution)/shard_map/add | solution.py:47
  394.2 7.1 %fusion.13 = f32[2048,8,128]{2,0,1:T(8,128)S(1)} fusion(f32[2,2048,8,128]{3,1,2,0:T(8,128)S(1)} %multiply_add_fusion, s32[128]{0:T(128)S(1)} %get-tuple-element.17, s32[128]{0:T(128)S(1)} %get-tuple-element.18), kind=kOutput, calls=%fused_computation.32 | convolution fusion | flops 3221487616 | bytes 16779264 | tf_op jit(solution)/shard_map/...k,gk->...g/dot_general | solution.py:58
  401.3 15.3 %fusion.10 = f32[2048,8,128]{2,0,1:T(8,128)S(1)} fusion(f32[2,2048,8,128]{3,1,2,0:T(8,128)S(1)} %multiply_add_fusion, s32[128]{0:T(128)S(1)} %get-tuple-element.17, s32[128]{0:T(128)S(1)} %get-tuple-element.18), kind=kOutput, calls=%fused_computation.29 | convolution fusion | flops 3221487616 | bytes 16779264 | tf_op jit(solution)/shard_map/...k,gk->...g/dot_general | solution.py:62
  416.6 9.0 %fusion.14 = bf16[1,2048,8,128]{3,1,2,0:T(8,128)(2,1)} fusion(f32[2048,8,128]{2,0,1:T(8,128)S(1)} %fusion.13, f32[2,2048,8,128]{3,1,2,0:T(8,128)S(1)} %multiply_add_fusion, s32[128]{0:T(128)S(1)} %get-tuple-element.17, s32[128]{0:T(128)S(1)} %get-tuple-element.18), kind=kOutput, calls=%fused_computation.33 | convolution fusion | flops 3227779072 | bytes 20973568 | tf_op jit(solution)/shard_map/...k,gk->...g/dot_general | solution.py:57
  425.6 9.0 %fusion.15 = bf16[1,2048,8,128]{3,1,2,0:T(8,128)(2,1)} fusion(f32[2048,8,128]{2,0,1:T(8,128)S(1)} %fusion.10, f32[2,2048,8,128]{3,1,2,0:T(8,128)S(1)} %multiply_add_fusion, s32[128]{0:T(128)S(1)} %get-tuple-element.17, s32[128]{0:T(128)S(1)} %get-tuple-element.18), kind=kOutput, calls=%fused_computation.34 | convolution fusion | flops 3227779072 | bytes 20973568 | tf_op jit(solution)/shard_map/...k,gk->...g/dot_general | solution.py:61
  434.6 11.8 %slice_bitcast_fusion = (bf16[8,256,1,2048]{3,1,2,0:T(8,128)(2,1)}, bf16[8,256,1,2048]{3,1,2,0:T(8,128)(2,1)}) fusion(bf16[2,8,256,2048]{3,2,1,0:T(8,128)(2,1)} %all-gather.2.cloned.1.call-done), kind=kLoop, calls=%fused_computation.18 | loop fusion | bytes 33554432 | tf_op jit(solution)/shard_map/squeeze | solution.py:74
  446.4 7.3 %fusion.64 = bf16[8,256,1,2048]{3,1,2,0:T(8,128)(2,1)} fusion(bf16[2,8,256,2048]{3,2,1,0:T(8,128)(2,1)} %all-gather.2.cloned.1.call-done), kind=kLoop, calls=%fused_computation.94 | loop fusion | flops 4194304 | bytes 16777216 | tf_op jit(solution)/shard_map/neg | solution.py:75
  453.7 0.0 copy-done
  453.7 0.0 copy-done.2
  453.7 18.0 %bitcast_multiply_fusion = f32[8,128,512]{2,1,0:T(8,128)} fusion(bf16[1,2048,8,128]{3,1,2,0:T(8,128)(2,1)} %fusion.15, bf16[1,2048,8,128]{3,1,2,0:T(8,128)(2,1)S(1)} %copy-done, f32[8]{0:T(128)S(1)} %copy-done.2, bf16[8,256,1,2048]{3,1,2,0:T(8,128)(2,1)} %get-tuple-element.6, bf16[8,256,1,2048]{3,1,2,0:T(8,128)(2,1)} %get-tuple-element.5, ...), kind=kOutput, calls=%fused_computation.35 | convolution fusion | flops 4433903616 | bytes 35651616 | tf_op jit(solution)/shard_map/cnpx,cypx->cny/dot_general | solution.py:78
  471.7 2.6 reshape.157
  474.3 1.6 copy.31
  (11 shorter events, 0.0 us)
Async XLA Ops:
  6.5 428.0 %all-gather.2.cloned.1.call-start = ((), (), s32[]{:S(2)}) async-start(), calls=%async_computation.1 | async-start | bytes 18874368 | tf_op jit(solution)/shard_map/all_gather | solution.py:94
  272.5 9.0 %copy-start.1 = (s32[4,16]{1,0:T(4,128)S(1)}, s32[4,16]{1,0:T(4,128)}, u32[]{:S(2)}) copy-start(s32[4,16]{1,0:T(4,128)} %param.9) | copy-start | bytes 772
  279.3 74.5 %collective-permute-start = (bf16[2,2048,8,48]{1,3,2,0:T(8,128)(2,1)S(1)}, bf16[2,2048,8,48]{1,3,2,0:T(8,128)(2,1)}, u32[]{:S(2)}, u32[]{:S(2)}) collective-permute-start(bf16[2,2048,8,48]{1,3,2,0:T(8,128)(2,1)S(1)} %copy.14), channel_id=1, source_target_pairs={{0,1},{1,2},{2,3},{3,4},{4,5},{5,6},{6,7},{8,9},{9,10},{10,11},{11... | collective-permute-start | bytes 9437192 | tf_op jit(solution)/shard_map/ppermute | solution.py:12
  446.4 7.3 %copy-start = (bf16[1,2048,8,128]{3,1,2,0:T(8,128)(2,1)S(1)}, bf16[1,2048,8,128]{3,1,2,0:T(8,128)(2,1)}, u32[]{:S(2)}) copy-start(bf16[1,2048,8,128]{3,1,2,0:T(8,128)(2,1)} %fusion.14) | copy-start | bytes 12582916
  446.4 7.3 %copy-start.2 = (f32[8]{0:T(128)S(1)}, f32[8]{0:T(128)}, u32[]{:S(2)}) copy-start(f32[8]{0:T(128)} %param.8) | copy-start | bytes 100
Sparse Core Ops, SparseCore 0:
  9.2 217.7 all-gather.1
where the time goes:
time: 490 us; the launch traced here: 483 us
  blocking collectives  217 us (44%)
  waiting for transfers between devices  72.7 us (15%)
  other arithmetic  64.5 us (13%)
  matrix products  58.4 us (12%)
  local copies, waits for them, and re-layouts  54.9 us (11%)
  between operations  13.7 us (3%)
    all_to_all x1, blocking collectives, shards(): lax.all_to_all(calibrated, 'chan', split_axis=2, concat_axis=1, tiled=True)  217 us
    ppermute x1, waiting for transfers between devices, from_behind(): return lax.ppermute(x, axis, pairs)  71.9 us
    add x1, other arithmetic, channelize(): filtered + jnp.tile(tap_coef[tap_index], span // length) * extended[...,...  32 us
    another operation x1, other arithmetic  18.7 us
    dot_general x1, matrix products, beam_terms(): jnp.einsum('cnpx,cypx->cny', spectra, panel_all, preferred_element_type=j...  18 us
    slice x2, local copies, waits for them, and re-layouts, shards(): prior_rim = from_behind(turned[..., turned.shape[-1] - halo_len:], 'tm', 1)  15.7 us
    dot_general x1, matrix products, channelize(): jnp.einsum('...k,gk->...g', filtered[0], sine_table, precision=highest)  15.3 us
    squeeze x1, local copies, waits for them, and re-layouts, beam_terms(): weight_im = weight[1]  11.8 us
  transfers between devices with their start and end apart: 2, of which 1 were waited for; matrix products, arithmetic and copies ran while one was open for 28% of the time, Pallas kernels for 0%

commit v1 on v0

v1 whole, which is shorter than its diff:
```python
import math

import jax
import jax.numpy as jnp
import numpy as np
from jax import lax
from jax.experimental import pallas as pl
from jax.experimental.pallas import tpu as pltpu
from jax.sharding import PartitionSpec as P

MESH = pl.DeviceIdType.MESH
F32 = jnp.float32
BF16 = jnp.bfloat16
NT = (((1,), (1,)), ((), ()))

INPUTS_HERE = 64
GROUP = 8
SPAN = 128
BEAMS = 256
LENGTH = 16
SPILL = 48
ROWS = 4 * SPAN + 2 * SPILL


def channelizer(fir_taps):
    sample = np.arange(SPAN)
    row = np.arange(SPAN + SPILL)
    lag = row[:, None] // LENGTH - sample[None, :] // LENGTH
    turn = (row[:, None] % LENGTH) * (sample[None, :] % LENGTH) % LENGTH
    angle = turn * (2.0 * math.pi / LENGTH)
    norm = 1.0 / (16.0 * math.sqrt(LENGTH))
    cos = jnp.asarray((np.cos(angle) * norm).astype(np.float32))
    sin = jnp.asarray((np.sin(angle) * norm).astype(np.float32))
    taps = jnp.tile(fir_taps.astype(F32), (1, SPAN // LENGTH))
    weight = jnp.zeros((SPAN + SPILL, SPAN), F32)
    for tap in range(fir_taps.shape[0]):
        weight = jnp.where(jnp.asarray(lag == tap), taps[tap][None, :], weight)
    cos, sin = cos * weight, sin * weight
    re = jnp.concatenate([cos, sin], axis=1)
    im = jnp.concatenate([-sin, cos], axis=1)
    full = jnp.concatenate([re[:SPAN], im[:SPAN], re[SPAN:], im[SPAN:]], axis=0)
    high = lax.reduce_precision(full, 8, 7)
    return jnp.concatenate([high, full - high], axis=0).astype(BF16)


def parity_split():
    q = np.arange(256)
    source = (q % 128) // 64 * 128 + (q // 128) * 64 + q % 64
    return jnp.asarray((np.arange(256)[:, None] == source[None, :]).astype(np.float32)).astype(BF16)


def kernel(
    v_ref, g_ref, w_ref, ct_ref, perm_ref, sc_ref, o_ref,
    vbuf, gbuf, wsplit, wbuf, spec, vf, xbuf, spf, osend, obuf, ssend, sbuf,
    v_send, v_recv, g_send, g_recv, w_send, w_recv, f_send, o_send, o_recv, s_send, s_recv,
):
    chan, tm = lax.axis_index("chan"), lax.axis_index("tm")
    xy, z = lax.div(chan, 2), lax.rem(chan, 2)
    t, k = lax.div(tm, 2), lax.rem(tm, 2)
    x, y = lax.div(xy, 4), lax.rem(xy, 4)
    u = lax.div(y, 2)
    differ = lax.rem(z + k, 2)

    def remote(src, dst, send, recv, to_chan, to_tm):
        return pltpu.make_async_remote_copy(
            src_ref=src, dst_ref=dst, send_sem=send, recv_sem=recv,
            device_id=(to_chan, to_tm), device_id_type=MESH,
        )

    def arrived(ref, sem):
        pltpu.make_async_copy(ref, ref, sem).wait()

    barrier = pltpu.get_barrier_semaphore()

    @pl.loop(1, 32)
    def _(n):
        other = lax.rem(xy * 2 + k + n, 32)
        pl.semaphore_signal(
            barrier, inc=1, device_id=(lax.div(other, 2) * 2 + z, t * 2 + lax.rem(other, 2)), device_id_type=MESH
        )

    @pl.loop(2, 16)
    def _(n):
        there = lax.rem(t * 2 + z + lax.div(n, 2), 8)
        pl.semaphore_signal(
            barrier, inc=1, device_id=(xy * 2 + lax.rem(there, 2), lax.div(there, 2) * 2 + lax.rem(n, 2)), device_id_type=MESH
        )

    pl.semaphore_wait(barrier, 31 + 14)

    def offsets(p):
        a = lax.div(p, 2)
        return a + lax.div(a, 2) - 2 * lax.div(a, 3), lax.rem(p, 2)

    def v_copies(p, e, k2):
        dx, du = offsets(p)
        to_xy = lax.rem(x - dx + 4, 4) * 4 + lax.rem(u + du, 2) * 2 + e
        group = to_xy * 2 + k2
        local = jnp.logical_and(to_xy == xy, k2 == k)
        far = remote(
            v_ref.at[:, :, group], vbuf.at[xy, k], v_send.at[group], v_recv.at[xy * 2 + k], to_xy * 2 + z, t * 2 + k2
        )
        near = pltpu.make_async_copy(v_ref.at[:, :, group], vbuf.at[xy, k], v_recv.at[xy * 2 + k])
        return local, far, near

    def g_copies(p, e):
        dx, du = offsets(p)
        to_xy = lax.rem(x - dx + 4, 4) * 4 + lax.rem(u + du, 2) * 2 + e
        far = remote(g_ref.at[to_xy * 2 + k], gbuf.at[xy], g_send.at[to_xy], g_recv.at[xy], to_xy * 2 + z, tm)
        near = pltpu.make_async_copy(g_ref.at[to_xy * 2 + k], gbuf.at[xy], g_recv.at[xy])
        return to_xy == xy, far, near

    def w_columns(slot):
        return pl.ds(pl.multiple_of(slot * 128, 128), 128)

    def w_copies(c):
        dst = wbuf.at[c, :, w_columns(tm)]
        sem = w_recv.at[c * 8 + tm]
        mine, others = wsplit.at[z, c], wsplit.at[1 - z, c]
        over = xy * 2 + 1 - z
        near = pltpu.make_async_copy(mine, dst, sem)
        sibling = remote(mine, dst, w_send.at[c * 5], sem, chan, t * 2 + z)
        far = [
            remote(others, dst, w_send.at[c * 5 + 1], sem, over, lax.rem(t + z, 4) * 2 + z),
            remote(others, dst, w_send.at[c * 5 + 2], sem, over, lax.rem(t + z + 3, 4) * 2 + z),
            remote(mine, dst, w_send.at[c * 5 + 3], sem, chan, lax.rem(t + 1, 4) * 2 + z),
            remote(mine, dst, w_send.at[c * 5 + 4], sem, chan, lax.rem(t + 3, 4) * 2 + z),
        ]
        return near, sibling, far

    behind = lax.rem(t + 3 + differ * z, 4)
    ahead = lax.rem(t + 1 - differ + differ * z, 4)

    def forward(c, slot, index, step):
        block = wbuf.at[c, :, w_columns(slot)]
        return remote(
            block, block, f_send.at[c * 4 + index], w_recv.at[c * 8 + slot], chan, lax.rem(t + 4 + step, 4) * 2 + k
        )

    def forwards(c):
        always = [forward(c, behind * 2, 0, 1), forward(c, ahead * 2 + 1, 1, -1)]
        crossed = [forward(c, behind * 2 + 1, 2, 1), forward(c, ahead * 2, 3, -1)]
        return always, crossed

    @pl.loop(0, 8)
    def _(c):
        both = jnp.concatenate([w_ref[0, c], w_ref[1, c]], axis=0)
        split = jnp.dot(both, perm_ref[...], preferred_element_type=F32).astype(BF16)
        wsplit[0, c] = split[:, :128]
        wsplit[1, c] = split[:, 128:]
        near, sibling, far = w_copies(c)
        for copy in far:
            copy.start()

        @pl.when(differ == 0)
        def _():
            near.start()

        @pl.when(differ == 1)
        def _():
            sibling.start()

        for e in range(2):
            here, far, near = g_copies(c, e)
            pl.when(here)(near.start)
            pl.when(jnp.logical_not(here))(far.start)
            for k2 in range(2):
                here, far, near = v_copies(c, e, k2)
                pl.when(here)(near.start)
                pl.when(jnp.logical_not(here))(far.start)

    @pl.loop(0, 8)
    def _(p):
        for slot in (behind * 2, behind * 2 + 1, ahead * 2, ahead * 2 + 1):
            arrived(wbuf.at[p, :, w_columns(slot)], w_recv.at[p * 8 + slot])
        always, crossed = forwards(p)
        for copy in always:
            copy.start()

        @pl.when(differ == 1)
        def _():
            for copy in crossed:
                copy.start()

        dx, du = offsets(p)
        pair = lax.rem(x + dx, 4) * 2 + lax.rem(u + du, 2)
        for e in range(2):
            arrived(gbuf.at[pair * 2 + e], g_recv.at[pair * 2 + e])
            for half in range(2):
                arrived(vbuf.at[pair * 2 + e, half], v_recv.at[pair * 4 + 2 * e + half])
        turned = [gbuf[pair * 2 + e].T for e in range(2)]
        gain_re = jnp.concatenate([turned[e][:64] for e in range(2)], axis=0)
        gain_im = jnp.concatenate([turned[e][64:] for e in range(2)], axis=0)
        columns = pl.ds(pl.multiple_of(pair * 128, 128), 128)
        for half in range(2):
            for part in range(2):
                for e in range(2):
                    vf[part, e * 512 : (e + 1) * 512] = (
                        vbuf[pair * 2 + e, half, part].astype(F32).reshape(512, 128)
                    )
            for c in range(8):
                volt_re, volt_im = (
                    jnp.concatenate(
                        [vf.at[part][pl.ds(e * 512 + c, 64, stride=8), :] for e in range(2)], axis=0
                    )
                    for part in range(2)
                )
                g_re, g_im = gain_re[:, c : c + 1], gain_im[:, c : c + 1]
                xbuf[c * 128 : (c + 1) * 128, :128] = (g_re * volt_re - g_im * volt_im).astype(BF16)
                xbuf[c * 128 : (c + 1) * 128, 128:] = (g_re * volt_im + g_im * volt_re).astype(BF16)

            @pl.loop(0, 4)
            def _(q):
                rows = xbuf[pl.ds(pl.multiple_of(q * 256, 256), 256)]
                made = lax.dot_general(ct_ref[...], rows, NT, preferred_element_type=F32)
                made = made[:352] + made[352:]
                re, im, tail = made[:128], made[128:256], made[256:]
                if half == 0:
                    spf[q] = tail
                else:
                    before = spf[q]
                    re = jnp.concatenate([re[:SPILL] + before[:SPILL], re[SPILL:]], axis=0)
                    im = jnp.concatenate([im[:SPILL] + before[SPILL:], im[SPILL:]], axis=0)
                for d in range(2):
                    lanes = slice(d * 128, (d + 1) * 128)
                    spec[q * 2 + d, half * 128 : half * 128 + 128, columns] = re[:, lanes].astype(BF16)
                    spec[q * 2 + d, 256 + half * 128 : 384 + half * 128, columns] = im[:, lanes].astype(BF16)
                    if half == 1:
                        spec[q * 2 + d, 512:ROWS, columns] = tail[:, lanes].astype(BF16)

    def o_copies(c, half):
        src, dst, sem = osend.at[c, half], obuf.at[c, z], o_recv.at[c * 2 + z]
        near = pltpu.make_async_copy(src, dst, sem)
        far = remote(src, dst, o_send.at[c * 2 + half], sem, xy * 2 + k, t * 2 + half)
        return jnp.logical_and(differ == 0, k == half), far, near

    def s_copy(c):
        return remote(ssend.at[c], sbuf.at[c, z], s_send.at[c], s_recv.at[c * 2 + z], xy * 2 + k, lax.rem(t + 1, 4) * 2)

    from_a = lax.rem(t + differ * (2 + z), 4)
    from_b = lax.rem(t + 2 - differ + differ * z, 4)

    def collect(c):
        for h in range(2):
            arrived(obuf.at[c, h], o_recv.at[c * 2 + h])
        scale = sc_ref[c]
        for part in range(2):
            o_ref[part, c] = (obuf[c, 0, part].astype(F32) + obuf[c, 1, part].astype(F32)) * scale

        @pl.when(jnp.logical_and(t > 0, k == 0))
        def _():
            for h in range(2):
                arrived(sbuf.at[c, h], s_recv.at[c * 2 + h])
            late = (sbuf[c, 0].astype(F32) + sbuf[c, 1].astype(F32)) * scale
            for part in range(2):
                o_ref[part, c, :SPILL] += late[part * SPILL : (part + 1) * SPILL]

    @pl.loop(0, 8)
    def _(c):
        for slot in (from_a * 2, from_a * 2 + 1, from_b * 2, from_b * 2 + 1):
            arrived(wbuf.at[c, :, w_columns(slot)], w_recv.at[c * 8 + slot])

        def sums(left):
            by_re = lax.dot_general(left, wbuf[c, :BEAMS], NT, preferred_element_type=F32)
            by_im = lax.dot_general(left, wbuf[c, BEAMS:], NT, preferred_element_type=F32)
            n = left.shape[0] // 2
            return (by_re[:n] - by_im[n:]).astype(BF16), (by_re[n:] + by_im[:n]).astype(BF16)

        for half in range(2):
            left = jnp.concatenate(
                [spec[c, half * 128 : half * 128 + 128], spec[c, 256 + half * 128 : 384 + half * 128]], axis=0
            )
            osend[c, half, 0], osend[c, half, 1] = sums(left)
            here, far, near = o_copies(c, half)
            pl.when(here)(near.start)
            pl.when(jnp.logical_not(here))(far.start)
        ssend[c, :SPILL], ssend[c, SPILL:] = sums(spec[c, 512:ROWS])

        @pl.when(t < 3)
        def _():
            s_copy(c).start()

        @pl.when(c > 0)
        def _():
            collect(c - 1)

    collect(7)

    @pl.loop(0, 8)
    def _(c):
        near, sibling, far = w_copies(c)
        for copy in far:
            copy.wait_send()
        always, crossed = forwards(c)
        for copy in always:
            copy.wait_send()

        @pl.when(differ == 1)
        def _():
            sibling.wait_send()
            for copy in crossed:
                copy.wait_send()

        for e in range(2):
            here, far, near = g_copies(c, e)
            pl.when(jnp.logical_not(here))(far.wait_send)
            for k2 in range(2):
                here, far, near = v_copies(c, e, k2)
                pl.when(jnp.logical_not(here))(far.wait_send)
        for half in range(2):
            here, far, near = o_copies(c, half)
            pl.when(jnp.logical_not(here))(far.wait_send)

        @pl.when(t < 3)
        def _():
            s_copy(c).wait_send()


def shards(voltages, channel_gains, weights, scales, fir_taps):
    volts = voltages.reshape(2, INPUTS_HERE, 32, GROUP, SPAN)
    gains = channel_gains.reshape(2 * INPUTS_HERE, 32 * GROUP).T.reshape(32, GROUP, 2 * INPUTS_HERE)
    vmem = pl.BlockSpec(memory_space=pltpu.VMEM)
    dma = pltpu.SemaphoreType.DMA
    formed = pl.pallas_call(
        kernel,
        out_shape=jax.ShapeDtypeStruct((2, GROUP, SPAN, BEAMS), F32),
        in_specs=[
            pl.BlockSpec(memory_space=pl.ANY),
            vmem,
            vmem,
            vmem,
            vmem,
            pl.BlockSpec(memory_space=pltpu.SMEM),
        ],
        out_specs=vmem,
        scratch_shapes=[
            pltpu.VMEM((16, 2, 2, INPUTS_HERE, GROUP, SPAN), BF16),
            pltpu.VMEM((16, GROUP, 2 * INPUTS_HERE), F32),
            pltpu.VMEM((2, GROUP, 2 * BEAMS, 128), BF16),
            pltpu.VMEM((GROUP, 2 * BEAMS, 1024), BF16),
            pltpu.VMEM((GROUP, ROWS, 1024), BF16),
            pltpu.VMEM((2, 1024, 128), F32),
            pltpu.VMEM((1024, 256), BF16),
            pltpu.VMEM((4, 2 * SPILL, 256), F32),
            pltpu.VMEM((GROUP, 2, 2, SPAN, BEAMS), BF16),
            pltpu.VMEM((GROUP, 2, 2, SPAN, BEAMS), BF16),
            pltpu.VMEM((GROUP, 2 * SPILL, BEAMS), BF16),
            pltpu.VMEM((GROUP, 2, 2 * SPILL, BEAMS), BF16),
            dma((32,)),
            dma((32,)),
            dma((16,)),
            dma((16,)),
            dma((40,)),
            dma((64,)),
            dma((32,)),
            dma((16,)),
            dma((16,)),
            dma((8,)),
            dma((16,)),
        ],
        compiler_params=pltpu.CompilerParams(
            collective_id=0, has_side_effects=True, vmem_limit_bytes=58 * 1024 * 1024
        ),
        cost_estimate=pl.CostEstimate(flops=20_000_000_000, bytes_accessed=15_000_000, transcendentals=0),
    )(volts, gains, weights, channelizer(fir_taps), parity_split(), scales)
    return formed.reshape(2, GROUP, SPAN // LENGTH, LENGTH, BEAMS)


def solution(mesh):
    in_specs = (
        P(None, "chan", None, "tm"),
        P(None, "chan", None),
        P(None, "chan", None, "tm"),
        P("chan"),
        P(),
    )
    out_specs = P(None, "chan", "tm", None, None)
    return jax.shard_map(shards, mesh=mesh, in_specs=in_specs, out_specs=out_specs, check_vma=False)
```

time: 490 us -> 236 us (0.48); the launches traced: 483 us -> 236 us
  Pallas kernels: 0 us -> 228 us
  blocking collectives: 217 us -> 0 us
  waiting for transfers between devices: 72.7 us -> 0 us
  other arithmetic: 64.5 us -> 2.56 us
  matrix products: 58.4 us -> 0 us
  local copies, waits for them, and re-layouts: 54.9 us -> 5.15 us
  between operations: 13.7 us -> 0.03 us
    pallas_call x0 -> x1, Pallas kernels: none -> 228 us  [shards(): pl.pallas_call(kernel, out_shape=jax.ShapeDtypeStruct((2, GROUP, SPAN, BE...]
    all_to_all x1 -> x0, blocking collectives: 217 us -> none  [shards(): lax.all_to_all(calibrated, 'chan', split_axis=2, concat_axis=1, tiled=True)]
    ppermute x1 -> x0, waiting for transfers between devices: 71.9 us -> none  [from_behind(): return lax.ppermute(x, axis, pairs)]
    dot_general x5 -> x0, matrix products: 58.4 us -> none  [the longest x1 18 us: beam_terms(): jnp.einsum('cnpx,cypx->cny', spectra, panel_all, preferred_element_type=j...]
    add x1 -> x0, other arithmetic: 32 us -> none  [channelize(): filtered + jnp.tile(tap_coef[tap_index], span // length) * extended[...,...]
    another operation x2 -> x1, other arithmetic: 25.1 us -> 0.05 us
    slice x3 -> x1, local copies, waits for them, and re-layouts: 19.7 us -> 0.01 us  [channelizer(): weight = jnp.where(jnp.asarray(lag == tap), taps[tap][None, :], weight)]
    squeeze x1 -> x0, local copies, waits for them, and re-layouts: 11.8 us -> none  [beam_terms(): weight_im = weight[1]]
  transfers between devices with their start and end apart: 2 -> 0, of which waited for: 1 -> 0; matrix products, arithmetic and copies ran while one was open for 28% -> 0% of each run, Pallas kernels for 0% -> 0%
where the time goes in v1:
time: 236 us
  Pallas kernels  228 us (97%)
  local copies, waits for them, and re-layouts  5.15 us (2%)
  other arithmetic  2.56 us (1%)
    pallas_call x1, Pallas kernels, shards(): pl.pallas_call(kernel, out_shape=jax.ShapeDtypeStruct((2, GROUP, SPAN, BE...  228 us

profile of v1, /device:TPU:170, one launch (start us, length us, event | category | flops | bytes accessed | tf_op | source)
XLA Modules:
  0.0 236.1 jit_solution(6562968713978860810)
XLA Ops:
  0.0 0.7 convert_element_type.7
  0.7 0.1 tile.22
  0.8 0.1 tile.28
  0.9 0.1 tile.26
  0.9 0.1 tile.24
  1.0 1.7 copy.13
  2.7 1.1 fusion.6
  3.8 0.8 pad_maximum_fusion.ct_ref
  4.6 228.4 %shard_map.118 = f32[2,8,128,256]{3,2,1,0:T(8,128)} custom-call(bf16[2,64,32,8,128]{4,3,2,1,0:T(8,128)(2,1)} %bitcast.17, f32[32,8,128]{2,1,0:T(8,128)} %bitcast.16, bf16[2,8,256,256]{3,2,1,0:T(8,128)(2,1)} %w_ref.1, bf16[704,256]{1,0:T(8,128)(2,1)} %pad_maximum_fusion.ct_ref, bf16[256,256]{1,0:T(8,128)(2,1)} %constant.25.perm_ref, f32[8]{0:T(128)} %sc_ref.1), custom_call_target="tpu_custom_call" | custom-call | flops 20000000000 | bytes 15000000 | tf_op jit(solution)/shard_map/pallas_call | solution.py:324
  233.0 3.1 %copy.15 = f32[2,8,8,16,256]{4,3,2,1,0:T(8,128)} copy(f32[2,8,8,16,256]{4,3,2,1,0:T(8,128)} %bitcast.14) | data formatting | bytes 4194304
  (7 shorter events, 0.1 us)

commit v2 on v1

v2 whole, which is shorter than its diff:
```python
import math

import jax
import jax.numpy as jnp
import ml_dtypes
import numpy as np
from jax import lax
from jax.experimental import pallas as pl
from jax.experimental.pallas import tpu as pltpu
from jax.sharding import PartitionSpec as P

MESH = pl.DeviceIdType.MESH
F32 = jnp.float32
BF16 = jnp.bfloat16
NT = (((1,), (1,)), ((), ()))

INPUTS_HERE = 64
GROUP = 8
SPAN = 128
BEAMS = 256
LENGTH = 16
SPILL = 48
ROWS = 4 * SPAN + 2 * SPILL


FRAMES = SPAN // LENGTH
LEAD = 8
SHIFTED = 3

NEAR = [(1, 0), (3, 0), (0, 1), (0, 3)]
FAR = [[(2, 0), (0, 2)], [(1, 1), (3, 3)], [(1, 3), (3, 1)], [(2, 1), (1, 2), (2, 3), (3, 2)], [(2, 2)]]
TARGETS = [(0, 0, 0), (0, 0, 1)] + [(dx, dy, dk) for run in [NEAR] + FAR for dk in range(2) for dx, dy in run]


def turns():
    product = np.arange(LENGTH)[:, None] * (np.arange(SPAN)[None, :] % LENGTH) % LENGTH
    angle = product * (2.0 * math.pi / LENGTH)
    norm = 1.0 / (16.0 * math.sqrt(LENGTH))
    return jnp.asarray(np.stack([np.cos(angle) * norm, np.sin(angle) * norm]).astype(np.float32))


def parity_split():
    q = np.arange(256)
    source = (q % 128) // 64 * 128 + (q // 128) * 64 + q % 64
    return jnp.asarray((np.arange(256)[:, None] == source[None, :]).astype(ml_dtypes.bfloat16))


def kernel(
    v_ref, g_ref, w_ref, turn_ref, perm_ref, taps_ref, sc_ref, o_ref,
    ct, gt, vbuf, gbuf, wsplit, wbuf, spec, vf, xbuf, spf, osend, obuf, ssend, sbuf,
    v_send, v_recv, g_send, g_recv, w_send, w_recv, f_send, o_send, o_recv, s_send, s_recv,
):
    chan, tm = lax.axis_index("chan"), lax.axis_index("tm")
    xy, z = lax.div(chan, 2), lax.rem(chan, 2)
    t, k = lax.div(tm, 2), lax.rem(tm, 2)
    x, y = lax.div(xy, 4), lax.rem(xy, 4)
    u = lax.div(y, 2)
    differ = lax.rem(z + k, 2)

    def remote(src, dst, send, recv, to_chan, to_tm):
        return pltpu.make_async_remote_copy(
            src_ref=src, dst_ref=dst, send_sem=send, recv_sem=recv,
            device_id=(to_chan, to_tm), device_id_type=MESH,
        )

    def arrived(ref, sem):
        pltpu.make_async_copy(ref, ref, sem).wait()

    barrier = pltpu.get_barrier_semaphore()

    @pl.loop(1, 32)
    def _(n):
        other = lax.rem(xy * 2 + k + n, 32)
        pl.semaphore_signal(
            barrier, inc=1, device_id=(lax.div(other, 2) * 2 + z, t * 2 + lax.rem(other, 2)), device_id_type=MESH
        )

    @pl.loop(2, 16)
    def _(n):
        there = lax.rem(t * 2 + z + lax.div(n, 2), 8)
        pl.semaphore_signal(
            barrier, inc=1, device_id=(xy * 2 + lax.rem(there, 2), lax.div(there, 2) * 2 + lax.rem(n, 2)), device_id_type=MESH
        )

    for n in range(2):
        gt[n * 16 : (n + 1) * 16] = g_ref[:, n * 128 : (n + 1) * 128].T.reshape(16, GROUP, 2 * INPUTS_HERE)
    lane = lax.broadcasted_iota(jnp.int32, (LENGTH, SPAN), 1)
    phase, frame = lax.rem(lane, LENGTH), lax.div(lane, LENGTH)
    taps = []
    for tap in range(4):
        values = jnp.zeros((LENGTH, SPAN), F32)
        for n in range(LENGTH):
            values = jnp.where(phase == n, taps_ref[tap, n].astype(F32), values)
        taps.append(values)
    cos, sin = turn_ref[0], turn_ref[1]
    for m in range(FRAMES + 3):
        taken = jnp.zeros((LENGTH, SPAN), F32)
        for tap in range(4):
            taken = jnp.where(frame == m - tap, taps[tap], taken)
        at_re, at_im = (m * 16, SPAN + m * 16) if m < FRAMES else (128 + m * 16, 128 + SPILL + m * 16)
        for at, left, right in ((at_re, cos * taken, sin * taken), (at_im, -sin * taken, cos * taken)):
            full = jnp.concatenate([left, right], axis=1)
            ct[at : at + 16] = full.astype(BF16)
            ct[352 + at : 368 + at] = (full - ct[at : at + 16].astype(F32)).astype(BF16)

    @pl.loop(0, 8)
    def _(c):
        both = jnp.concatenate([w_ref[0, c], w_ref[1, c]], axis=0)
        split = jnp.dot(both, perm_ref[...], preferred_element_type=F32).astype(BF16)
        wsplit[0, c] = split[:, :128]
        wsplit[1, c] = split[:, 128:]

    pl.semaphore_wait(barrier, 31 + 14)

    def v_copy(dx, dy, dk):
        to_xy = lax.rem(x + dx, 4) * 4 + lax.rem(y + dy, 4)
        to_k = lax.rem(k + dk, 2)
        group = to_xy * 2 + to_k
        src, dst, sem = v_ref.at[:, :, group], vbuf.at[xy, k], v_recv.at[xy * 2 + k]
        if (dx, dy, dk) == (0, 0, 0):
            return pltpu.make_async_copy(src, dst, sem)
        return remote(src, dst, v_send.at[group], sem, to_xy * 2 + z, t * 2 + to_k)

    def g_copy(dx, dy):
        to_xy = lax.rem(x + dx, 4) * 4 + lax.rem(y + dy, 4)
        src, dst, sem = gt.at[to_xy * 2 + k], gbuf.at[xy], g_recv.at[xy]
        if (dx, dy) == (0, 0):
            return pltpu.make_async_copy(src, dst, sem)
        return remote(src, dst, g_send.at[to_xy], sem, to_xy * 2 + z, tm)

    def w_columns(slot):
        return pl.ds(pl.multiple_of(slot * 128, 128), 128)

    def w_near(c):
        return pltpu.make_async_copy(wsplit.at[z, c], wbuf.at[c, :, w_columns(tm)], w_recv.at[c * 8 + tm])

    def w_copy(c, index):
        mine, others = wsplit.at[z, c], wsplit.at[1 - z, c]
        over = xy * 2 + 1 - z
        src, to_chan, to_t = [
            (mine, chan, t),
            (others, over, lax.rem(t + z, 4)),
            (others, over, lax.rem(t + z + 3, 4)),
            (mine, chan, lax.rem(t + 1, 4)),
            (mine, chan, lax.rem(t + 3, 4)),
        ][index]
        return remote(
            src, wbuf.at[c, :, w_columns(tm)], w_send.at[c * 5 + index], w_recv.at[c * 8 + tm], to_chan, to_t * 2 + z
        )

    def send_weights(c):
        for index in range(1, 5):
            w_copy(c, index).start()

        @pl.when(differ == 0)
        def _():
            w_near(c).start()

        @pl.when(differ == 1)
        def _():
            w_copy(c, 0).start()

    behind = lax.rem(t + 3 + differ * z, 4)
    ahead = lax.rem(t + 1 - differ + differ * z, 4)

    def forward(c, slot, index, step):
        block = wbuf.at[c, :, w_columns(slot)]
        return remote(
            block, block, f_send.at[c * 4 + index], w_recv.at[c * 8 + slot], chan, lax.rem(t + 4 + step, 4) * 2 + k
        )

    def forwards(c):
        shift = (1 - differ) * (1 - lax.div(c + 8 - SHIFTED, 8))
        return [
            lambda: forward(c, (behind + shift * (ahead - behind)) * 2, 0, 1 - 2 * shift),
            lambda: forward(c, ahead * 2 + 1, 1, -1),
        ]

    def crossed(c):
        return [lambda: forward(c, behind * 2 + 1, 2, 1), lambda: forward(c, ahead * 2, 3, -1)]

    def pass_on(c):
        for slot in (behind * 2, behind * 2 + 1, ahead * 2, ahead * 2 + 1):
            arrived(wbuf.at[c, :, w_columns(slot)], w_recv.at[c * 8 + slot])
        for copy in forwards(c):
            copy().start()

        @pl.when(differ == 1)
        def _():
            for copy in crossed(c):
                copy().start()

        @pl.when(c + LEAD < 8)
        def _():
            send_weights(c + LEAD)

    @pl.loop(0, LEAD)
    def _(c):
        send_weights(c)

    for dx, dy, dk in TARGETS:
        if dk == 0:
            g_copy(dx, dy).start()
        v_copy(dx, dy, dk).start()

    @pl.loop(0, 8)
    def _(p):
        m = lax.div(p + 2, 4)
        odd = lax.rem(p, 2)
        dx = m + lax.rem(m, 2) * 2 * odd
        du = (1 - lax.rem(m, 2)) * odd + lax.rem(m, 2) * lax.div(p, 4)
        pair = lax.rem(x + dx, 4) * 2 + lax.rem(u + du, 2)
        for e in range(2):
            arrived(gbuf.at[pair * 2 + e], g_recv.at[pair * 2 + e])
            for half in range(2):
                arrived(vbuf.at[pair * 2 + e, half], v_recv.at[pair * 4 + 2 * e + half])
        turned = [gbuf[pair * 2 + e].T for e in range(2)]
        gain_re = jnp.concatenate([turned[e][:64] for e in range(2)], axis=0)
        gain_im = jnp.concatenate([turned[e][64:] for e in range(2)], axis=0)
        columns = pl.ds(pl.multiple_of(pair * 128, 128), 128)
        for half in range(2):
            for part in range(2):
                for e in range(2):
                    vf[part, e * 512 : (e + 1) * 512] = (
                        vbuf[pair * 2 + e, half, part].astype(F32).reshape(512, 128)
                    )
            for c in range(8):
                volt_re, volt_im = (
                    jnp.concatenate(
                        [vf.at[part][pl.ds(e * 512 + c, 64, stride=8), :] for e in range(2)], axis=0
                    )
                    for part in range(2)
                )
                g_re, g_im = gain_re[:, c : c + 1], gain_im[:, c : c + 1]
                xbuf[c * 128 : (c + 1) * 128, :128] = (g_re * volt_re - g_im * volt_im).astype(BF16)
                xbuf[c * 128 : (c + 1) * 128, 128:] = (g_re * volt_im + g_im * volt_re).astype(BF16)

            @pl.loop(0, 4)
            def _(q):
                rows = xbuf[pl.ds(pl.multiple_of(q * 256, 256), 256)]
                made = lax.dot_general(ct[...], rows, NT, preferred_element_type=F32)
                made = made[:352] + made[352:]
                re, im, tail = made[:128], made[128:256], made[256:]
                if half == 0:
                    spf[q] = tail
                else:
                    before = spf[q]
                    re = jnp.concatenate([re[:SPILL] + before[:SPILL], re[SPILL:]], axis=0)
                    im = jnp.concatenate([im[:SPILL] + before[SPILL:], im[SPILL:]], axis=0)
                for d in range(2):
                    lanes = slice(d * 128, (d + 1) * 128)
                    spec[q * 2 + d, half * 128 : half * 128 + 128, columns] = re[:, lanes].astype(BF16)
                    spec[q * 2 + d, 256 + half * 128 : 384 + half * 128, columns] = im[:, lanes].astype(BF16)
                    if half == 1:
                        spec[q * 2 + d, 512:ROWS, columns] = tail[:, lanes].astype(BF16)

        @pl.when(p < 6)
        def _():
            pass_on(p)

    def o_copies(c, half):
        src, dst, sem = osend.at[c, half], obuf.at[c, z], o_recv.at[c * 2 + z]
        here = jnp.logical_and(differ == 0, k == half)
        return (
            here,
            lambda: remote(src, dst, o_send.at[c * 2 + half], sem, xy * 2 + k, t * 2 + half),
            lambda: pltpu.make_async_copy(src, dst, sem),
        )

    def s_copy(c):
        return remote(ssend.at[c], sbuf.at[c, z], s_send.at[c], s_recv.at[c * 2 + z], xy * 2 + k, lax.rem(t + 1, 4) * 2)

    from_a = lax.rem(t + differ * (2 + z), 4)
    from_b = lax.rem(t + 2 - differ + differ * z, 4)

    def collect(c):
        for h in range(2):
            arrived(obuf.at[c, h], o_recv.at[c * 2 + h])
        scale = sc_ref[c]
        for part in range(2):
            o_ref[part, c] = (obuf[c, 0, part].astype(F32) + obuf[c, 1, part].astype(F32)) * scale

        @pl.when(jnp.logical_and(t > 0, k == 0))
        def _():
            for h in range(2):
                arrived(sbuf.at[c, h], s_recv.at[c * 2 + h])
            late = (sbuf[c, 0].astype(F32) + sbuf[c, 1].astype(F32)) * scale
            for part in range(2):
                o_ref[part, c, :SPILL] += late[part * SPILL : (part + 1) * SPILL]

    @pl.loop(0, 8)
    def _(c):
        for slot in (from_a * 2, from_a * 2 + 1, from_b * 2, from_b * 2 + 1):
            arrived(wbuf.at[c, :, w_columns(slot)], w_recv.at[c * 8 + slot])

        def sums(left):
            by_re = lax.dot_general(left, wbuf[c, :BEAMS], NT, preferred_element_type=F32)
            by_im = lax.dot_general(left, wbuf[c, BEAMS:], NT, preferred_element_type=F32)
            n = left.shape[0] // 2
            return (by_re[:n] - by_im[n:]).astype(BF16), (by_re[n:] + by_im[:n]).astype(BF16)

        for half in range(2):
            left = jnp.concatenate(
                [spec[c, half * 128 : half * 128 + 128], spec[c, 256 + half * 128 : 384 + half * 128]], axis=0
            )
            osend[c, half, 0], osend[c, half, 1] = sums(left)
            here, far, near = o_copies(c, half)
            pl.when(here)(lambda near=near: near().start())
            pl.when(jnp.logical_not(here))(lambda far=far: far().start())
        ssend[c, :SPILL], ssend[c, SPILL:] = sums(spec[c, 512:ROWS])

        @pl.when(t < 3)
        def _():
            s_copy(c).start()

        @pl.when(c > 0)
        def _():
            collect(c - 1)

        @pl.when(lax.rem(c, 3) == 2)
        def _():
            pass_on(6 + lax.div(c - 2, 3))

    collect(7)

    for dx, dy, dk in TARGETS[1:]:
        v_copy(dx, dy, dk).wait_send()
        if dk == 0:
            g_copy(dx, dy).wait_send()

    @pl.loop(0, 8)
    def _(c):
        for index in range(1, 5):
            w_copy(c, index).wait_send()
        for copy in forwards(c):
            copy().wait_send()

        @pl.when(differ == 1)
        def _():
            w_copy(c, 0).wait_send()
            for copy in crossed(c):
                copy().wait_send()

        for half in range(2):
            here, far, near = o_copies(c, half)
            pl.when(jnp.logical_not(here))(lambda far=far: far().wait_send())

        @pl.when(t < 3)
        def _():
            s_copy(c).wait_send()


def shards(voltages, channel_gains, weights, scales, fir_taps):
    volts = voltages.reshape(2, INPUTS_HERE, 32, GROUP, SPAN)
    gains = channel_gains.reshape(2 * INPUTS_HERE, 32 * GROUP)
    vmem = pl.BlockSpec(memory_space=pltpu.VMEM)
    dma = pltpu.SemaphoreType.DMA
    formed = pl.pallas_call(
        kernel,
        out_shape=jax.ShapeDtypeStruct((2, GROUP, SPAN, BEAMS), F32),
        in_specs=[
            pl.BlockSpec(memory_space=pl.ANY),
            vmem,
            vmem,
            vmem,
            vmem,
            pl.BlockSpec(memory_space=pltpu.SMEM),
            pl.BlockSpec(memory_space=pltpu.SMEM),
        ],
        out_specs=vmem,
        scratch_shapes=[
            pltpu.VMEM((704, 256), BF16),
            pltpu.VMEM((32, GROUP, 2 * INPUTS_HERE), F32),
            pltpu.VMEM((16, 2, 2, INPUTS_HERE, GROUP, SPAN), BF16),
            pltpu.VMEM((16, GROUP, 2 * INPUTS_HERE), F32),
            pltpu.VMEM((2, GROUP, 2 * BEAMS, 128), BF16),
            pltpu.VMEM((GROUP, 2 * BEAMS, 1024), BF16),
            pltpu.VMEM((GROUP, ROWS, 1024), BF16),
            pltpu.VMEM((2, 1024, 128), F32),
            pltpu.VMEM((1024, 256), BF16),
            pltpu.VMEM((4, 2 * SPILL, 256), F32),
            pltpu.VMEM((GROUP, 2, 2, SPAN, BEAMS), BF16),
            pltpu.VMEM((GROUP, 2, 2, SPAN, BEAMS), BF16),
            pltpu.VMEM((GROUP, 2 * SPILL, BEAMS), BF16),
            pltpu.VMEM((GROUP, 2, 2 * SPILL, BEAMS), BF16),
            dma((32,)),
            dma((32,)),
            dma((16,)),
            dma((16,)),
            dma((40,)),
            dma((64,)),
            dma((32,)),
            dma((16,)),
            dma((16,)),
            dma((8,)),
            dma((16,)),
        ],
        compiler_params=pltpu.CompilerParams(
            collective_id=0, has_side_effects=True, vmem_limit_bytes=58 * 1024 * 1024
        ),
        cost_estimate=pl.CostEstimate(flops=20_000_000_000, bytes_accessed=15_000_000, transcendentals=0),
    )(volts, gains, weights, turns(), parity_split(), fir_taps, scales)
    return formed.reshape(2, GROUP, SPAN // LENGTH, LENGTH, BEAMS)


def solution(mesh):
    in_specs = (
        P(None, "chan", None, "tm"),
        P(None, "chan", None),
        P(None, "chan", None, "tm"),
        P("chan"),
        P(),
    )
    out_specs = P(None, "chan", "tm", None, None)
    return jax.shard_map(shards, mesh=mesh, in_specs=in_specs, out_specs=out_specs, check_vma=False)
```

time: 236 us -> 199 us (0.84)
  the two profiles are of different devices: /device:TPU:170 before, /device:TPU:141 now
where the time goes in v2:
time: 199 us
  Pallas kernels  195 us (98%)
  local copies, waits for them, and re-layouts  3.14 us (2%)
    pallas_call x1, Pallas kernels, shards(): pl.pallas_call(kernel, out_shape=jax.ShapeDtypeStruct((2, GROUP, SPAN, BE...  195 us

profile of v2, /device:TPU:141, one launch (start us, length us, event | category | flops | bytes accessed | tf_op | source)
XLA Modules:
  0.0 198.6 jit_solution(1876747143783101924)
XLA Ops:
  0.0 195.4 %shard_map.73 = f32[2,8,128,256]{3,2,1,0:T(8,128)} custom-call(bf16[2,64,32,8,128]{4,3,2,1,0:T(8,128)(2,1)} %bitcast.4, f32[128,256]{1,0:T(8,128)} %bitcast.5, bf16[2,8,256,256]{3,2,1,0:T(8,128)(2,1)} %w_ref.1, f32[2,16,128]{2,1,0:T(8,128)} %constant.4.clone.turn_ref, bf16[256,256]{1,0:T(8,128)(2,1)} %constant.5.clone.perm_ref, s32[4,16]{1,0:T(4,128)} %taps_ref.1, ...), custom_call_target="tpu_custom_call" | custom-call | flops 20000000000 | bytes 15000000 | tf_op jit(solution)/shard_map/pallas_call | solution.py:358
  195.4 3.1 %copy.9 = f32[2,8,8,16,256]{4,3,2,1,0:T(8,128)} copy(f32[2,8,8,16,256]{4,3,2,1,0:T(8,128)} %bitcast.3) | data formatting | bytes 4194304

commit v3 on v2

--- a/solution.py
+++ b/solution.py
@@ -24,12 +24,18 @@
 
 
 FRAMES = SPAN // LENGTH
-LEAD = 8
-SHIFTED = 3
-
-NEAR = [(1, 0), (3, 0), (0, 1), (0, 3)]
-FAR = [[(2, 0), (0, 2)], [(1, 1), (3, 3)], [(1, 3), (3, 1)], [(2, 1), (1, 2), (2, 3), (3, 2)], [(2, 2)]]
-TARGETS = [(0, 0, 0), (0, 0, 1)] + [(dx, dy, dk) for run in [NEAR] + FAR for dk in range(2) for dx, dy in run]
+PASSED = [(0, 3), (3, 8)]
+SHIFTED = 1
+
+RUNS = [
+    [(2, 1), (0, 3), (2, 3), (0, 1)],
+    [(1, 2), (3, 0), (3, 2), (1, 0)],
+    [(1, 1), (3, 3)],
+    [(1, 3), (3, 1)],
+    [(2, 0), (0, 2)],
+    [(2, 2)],
+]
+TARGETS = [(0, 0, 0), (0, 0, 1)] + [(dx, dy, dk) for run in RUNS for dx, dy in run for dk in range(2)]
 
 
 def turns():
@@ -47,8 +53,8 @@
 
 def kernel(
     v_ref, g_ref, w_ref, turn_ref, perm_ref, taps_ref, sc_ref, o_ref,
-    ct, gt, vbuf, gbuf, wsplit, wbuf, spec, vf, xbuf, spf, osend, obuf, ssend, sbuf,
-    v_send, v_recv, g_send, g_recv, w_send, w_recv, f_send, o_send, o_recv, s_send, s_recv,
+    wv, ct, gt, vbuf, gbuf, wsplit, wbuf, spec, vf, xbuf, spf, osend, obuf, ssend, sbuf,
+    v_send, v_recv, g_send, g_recv, w_load, w_send, w_recv, f_send, o_send, o_recv, s_send, s_recv,
 ):
     chan, tm = lax.axis_index("chan"), lax.axis_index("tm")
     xy, z = lax.div(chan, 2), lax.rem(chan, 2)
@@ -66,6 +72,8 @@
     def arrived(ref, sem):
         pltpu.make_async_copy(ref, ref, sem).wait()
 
+    pltpu.make_async_copy(w_ref, wv, w_load).start()
+
     barrier = pltpu.get_barrier_semaphore()
 
     @pl.loop(1, 32)
@@ -82,8 +90,109 @@
             barrier, inc=1, device_id=(xy * 2 + lax.rem(there, 2), lax.div(there, 2) * 2 + lax.rem(n, 2)), device_id_type=MESH
         )
 
+    def split(c):
+        both = jnp.concatenate([wv[0, c], wv[1, c]], axis=0)
+        turned = jnp.dot(both, perm_ref[...], preferred_element_type=F32).astype(BF16)
+        wsplit[0, c] = turned[:, :128]
+        wsplit[1, c] = turned[:, 128:]
+
+    pltpu.make_async_copy(w_ref, wv, w_load).wait()
+    split(0)
+    pl.semaphore_wait(barrier, 31 + 14)
+
+    def v_copy(dx, dy, dk):
+        to_xy = lax.rem(x + dx, 4) * 4 + lax.rem(y + dy, 4)
+        to_k = lax.rem(k + dk, 2)
+        group = to_xy * 2 + to_k
+        src, dst, sem = v_ref.at[:, :, group], vbuf.at[xy, k], v_recv.at[xy * 2 + k]
+        if (dx, dy, dk) == (0, 0, 0):
+            return pltpu.make_async_copy(src, dst, sem)
+        return remote(src, dst, v_send.at[group], sem, to_xy * 2 + z, t * 2 + to_k)
+
+    def g_copy(dx, dy):
+        to_xy = lax.rem(x + dx, 4) * 4 + lax.rem(y + dy, 4)
+        src, dst, sem = gt.at[to_xy * 2 + k], gbuf.at[xy], g_recv.at[xy]
+        if (dx, dy) == (0, 0):
+            return pltpu.make_async_copy(src, dst, sem)
+        return remote(src, dst, g_send.at[to_xy], sem, to_xy * 2 + z, tm)
+
+    def w_columns(slot):
+        return pl.ds(pl.multiple_of(slot * 128, 128), 128)
+
+    def w_near(c):
+        return pltpu.make_async_copy(wsplit.at[z, c], wbuf.at[c, :, w_columns(tm)], w_recv.at[c * 8 + tm])
+
+    def w_copy(c, index):
+        mine, others = wsplit.at[z, c], wsplit.at[1 - z, c]
+        over = xy * 2 + 1 - z
+        src, to_chan, to_t = [
+            (mine, chan, t),
+            (others, over, lax.rem(t + z, 4)),
+            (others, over, lax.rem(t + z + 3, 4)),
+            (mine, chan, lax.rem(t + 1, 4)),
+            (mine, chan, lax.rem(t + 3, 4)),
+        ][index]
+        return remote(
+            src, wbuf.at[c, :, w_columns(tm)], w_send.at[c * 5 + index], w_recv.at[c * 8 + tm], to_chan, to_t * 2 + z
+        )
+
+    def send_weights(c):
+        for index in range(1, 5):
+            w_copy(c, index).start()
+
+        @pl.when(differ == 0)
+        def _():
+            w_near(c).start()
+
+        @pl.when(differ == 1)
+        def _():
+            w_copy(c, 0).start()
+
+    behind = lax.rem(t + 3 + differ * z, 4)
+    ahead = lax.rem(t + 1 - differ + differ * z, 4)
+
+    def forward(c, slot, index, step):
+        block = wbuf.at[c, :, w_columns(slot)]
+        return remote(
+            block, block, f_send.at[c * 4 + index], w_recv.at[c * 8 + slot], chan, lax.rem(t + 4 + step, 4) * 2 + k
+        )
+
+    def forwards(c):
+        shift = (1 - differ) * (1 - lax.div(c + 8 - SHIFTED, 8))
+        return [
+            lambda: forward(c, (behind + shift * (ahead - behind)) * 2, 0, 1 - 2 * shift),
+            lambda: forward(c, ahead * 2 + 1, 1, -1),
+        ]
+
+    def crossed(c):
+        return [lambda: forward(c, behind * 2 + 1, 2, 1), lambda: forward(c, ahead * 2, 3, -1)]
+
+    def pass_on(c):
+        for slot in (behind * 2, behind * 2 + 1, ahead * 2, ahead * 2 + 1):
+            arrived(wbuf.at[c, :, w_columns(slot)], w_recv.at[c * 8 + slot])
+        for copy in forwards(c):
+            copy().start()
+
+        @pl.when(differ == 1)
+        def _():
+            for copy in crossed(c):
+                copy().start()
+
+    send_weights(0)
+    for dx, dy, dk in TARGETS:
+        v_copy(dx, dy, dk).start()
+
+    @pl.loop(1, 8)
+    def _(c):
+        split(c)
+        send_weights(c)
+
     for n in range(2):
         gt[n * 16 : (n + 1) * 16] = g_ref[:, n * 128 : (n + 1) * 128].T.reshape(16, GROUP, 2 * INPUTS_HERE)
+    for dx, dy, dk in TARGETS:
+        if dk == 0:
+            g_copy(dx, dy).start()
+
     lane = lax.broadcasted_iota(jnp.int32, (LENGTH, SPAN), 1)
     phase, frame = lax.rem(lane, LENGTH), lax.div(lane, LENGTH)
     taps = []
@@ -104,111 +213,13 @@
             ct[352 + at : 368 + at] = (full - ct[at : at + 16].astype(F32)).astype(BF16)
 
     @pl.loop(0, 8)
-    def _(c):
-        both = jnp.concatenate([w_ref[0, c], w_ref[1, c]], axis=0)
-        split = jnp.dot(both, perm_ref[...], preferred_element_type=F32).astype(BF16)
-        wsplit[0, c] = split[:, :128]
-        wsplit[1, c] = split[:, 128:]
-
-    pl.semaphore_wait(barrier, 31 + 14)
-
-    def v_copy(dx, dy, dk):
-        to_xy = lax.rem(x + dx, 4) * 4 + lax.rem(y + dy, 4)
-        to_k = lax.rem(k + dk, 2)
-        group = to_xy * 2 + to_k
-        src, dst, sem = v_ref.at[:, :, group], vbuf.at[xy, k], v_recv.at[xy * 2 + k]
-        if (dx, dy, dk) == (0, 0, 0):
-            return pltpu.make_async_copy(src, dst, sem)
-        return remote(src, dst, v_send.at[group], sem, to_xy * 2 + z, t * 2 + to_k)
-
-    def g_copy(dx, dy):
-        to_xy = lax.rem(x + dx, 4) * 4 + lax.rem(y + dy, 4)
-        src, dst, sem = gt.at[to_xy * 2 + k], gbuf.at[xy], g_recv.at[xy]
-        if (dx, dy) == (0, 0):
-            return pltpu.make_async_copy(src, dst, sem)
-        return remote(src, dst, g_send.at[to_xy], sem, to_xy * 2 + z, tm)
-
-    def w_columns(slot):
-        return pl.ds(pl.multiple_of(slot * 128, 128), 128)
-
-    def w_near(c):
-        return pltpu.make_async_copy(wsplit.at[z, c], wbuf.at[c, :, w_columns(tm)], w_recv.at[c * 8 + tm])
-
-    def w_copy(c, index):
-        mine, others = wsplit.at[z, c], wsplit.at[1 - z, c]
-        over = xy * 2 + 1 - z
-        src, to_chan, to_t = [
-            (mine, chan, t),
-            (others, over, lax.rem(t + z, 4)),
-            (others, over, lax.rem(t + z + 3, 4)),
-            (mine, chan, lax.rem(t + 1, 4)),
-            (mine, chan, lax.rem(t + 3, 4)),
-        ][index]
-        return remote(
-            src, wbuf.at[c, :, w_columns(tm)], w_send.at[c * 5 + index], w_recv.at[c * 8 + tm], to_chan, to_t * 2 + z
-        )
-
-    def send_weights(c):
-        for index in range(1, 5):
-            w_copy(c, index).start()
-
-        @pl.when(differ == 0)
-        def _():
-            w_near(c).start()
-
-        @pl.when(differ == 1)
-        def _():
-            w_copy(c, 0).start()
-
-    behind = lax.rem(t + 3 + differ * z, 4)
-    ahead = lax.rem(t + 1 - differ + differ * z, 4)
-
-    def forward(c, slot, index, step):
-        block = wbuf.at[c, :, w_columns(slot)]
-        return remote(
-            block, block, f_send.at[c * 4 + index], w_recv.at[c * 8 + slot], chan, lax.rem(t + 4 + step, 4) * 2 + k
-        )
-
-    def forwards(c):
-        shift = (1 - differ) * (1 - lax.div(c + 8 - SHIFTED, 8))
-        return [
-            lambda: forward(c, (behind + shift * (ahead - behind)) * 2, 0, 1 - 2 * shift),
-            lambda: forward(c, ahead * 2 + 1, 1, -1),
-        ]
-
-    def crossed(c):
-        return [lambda: forward(c, behind * 2 + 1, 2, 1), lambda: forward(c, ahead * 2, 3, -1)]
-
-    def pass_on(c):
-        for slot in (behind * 2, behind * 2 + 1, ahead * 2, ahead * 2 + 1):
-            arrived(wbuf.at[c, :, w_columns(slot)], w_recv.at[c * 8 + slot])
-        for copy in forwards(c):
-            copy().start()
-
-        @pl.when(differ == 1)
-        def _():
-            for copy in crossed(c):
-                copy().start()
-
-        @pl.when(c + LEAD < 8)
-        def _():
-            send_weights(c + LEAD)
-
-    @pl.loop(0, LEAD)
-    def _(c):
-        send_weights(c)
-
-    for dx, dy, dk in TARGETS:
-        if dk == 0:
-            g_copy(dx, dy).start()
-        v_copy(dx, dy, dk).start()
-
-    @pl.loop(0, 8)
     def _(p):
-        m = lax.div(p + 2, 4)
-        odd = lax.rem(p, 2)
-        dx = m + lax.rem(m, 2) * 2 * odd
-        du = (1 - lax.rem(m, 2)) * odd + lax.rem(m, 2) * lax.div(p, 4)
+        for step, (first, last) in enumerate(PASSED):
+            pl.when(p == step)(lambda first=first, last=last: pl.loop(first, last)(pass_on))
+
+        m = lax.rem(lax.div(p + 3, 4), 2)
+        dx = m * (3 - 2 * lax.rem(p, 2)) + 2 * lax.div(p, 6)
+        du = lax.rem(lax.div(p, 3) + lax.div(p, 7), 2)
         pair = lax.rem(x + dx, 4) * 2 + lax.rem(u + du, 2)
         for e in range(2):
             arrived(gbuf.at[pair * 2 + e], g_recv.at[pair * 2 + e])
@@ -254,10 +265,6 @@
                     if half == 1:
                         spec[q * 2 + d, 512:ROWS, columns] = tail[:, lanes].astype(BF16)
 
-        @pl.when(p < 6)
-        def _():
-            pass_on(p)
-
     def o_copies(c, half):
         src, dst, sem = osend.at[c, half], obuf.at[c, z], o_recv.at[c * 2 + z]
         here = jnp.logical_and(differ == 0, k == half)
@@ -298,6 +305,12 @@
             by_im = lax.dot_general(left, wbuf[c, BEAMS:], NT, preferred_element_type=F32)
             n = left.shape[0] // 2
             return (by_re[:n] - by_im[n:]).astype(BF16), (by_re[n:] + by_im[:n]).astype(BF16)
+
+        ssend[c, :SPILL], ssend[c, SPILL:] = sums(spec[c, 512:ROWS])
+
+        @pl.when(t < 3)
+        def _():
+            s_copy(c).start()
 
         for half in range(2):
             left = jnp.concatenate(
@@ -307,19 +320,11 @@
             here, far, near = o_copies(c, half)
             pl.when(here)(lambda near=near: near().start())
             pl.when(jnp.logical_not(here))(lambda far=far: far().start())
-        ssend[c, :SPILL], ssend[c, SPILL:] = sums(spec[c, 512:ROWS])
-
-        @pl.when(t < 3)
-        def _():
-            s_copy(c).start()
 
         @pl.when(c > 0)
         def _():
             collect(c - 1)
 
-        @pl.when(lax.rem(c, 3) == 2)
-        def _():
-            pass_on(6 + lax.div(c - 2, 3))
 
     collect(7)
 
@@ -361,7 +366,7 @@
         in_specs=[
             pl.BlockSpec(memory_space=pl.ANY),
             vmem,
-            vmem,
+            pl.BlockSpec(memory_space=pl.ANY),
             vmem,
             vmem,
             pl.BlockSpec(memory_space=pltpu.SMEM),
@@ -369,6 +374,7 @@
         ],
         out_specs=vmem,
         scratch_shapes=[
+            pltpu.VMEM((2, GROUP, BEAMS, 256), BF16),
             pltpu.VMEM((704, 256), BF16),
             pltpu.VMEM((32, GROUP, 2 * INPUTS_HERE), F32),
             pltpu.VMEM((16, 2, 2, INPUTS_HERE, GROUP, SPAN), BF16),
@@ -387,6 +393,7 @@
             dma((32,)),
             dma((16,)),
             dma((16,)),
+            dma,
             dma((40,)),
             dma((64,)),
             dma((32,)),

time: 199 us -> 188 us (0.945)
  the two profiles are of different devices: /device:TPU:141 before, /device:TPU:170 now
where the time goes in v3:
time: 188 us; the launch traced here: 185 us
  Pallas kernels  182 us (97%)
  local copies, waits for them, and re-layouts  3.14 us (2%)
    pallas_call x1, Pallas kernels, shards(): pl.pallas_call(kernel, out_shape=jax.ShapeDtypeStruct((2, GROUP, SPAN, BE...  182 us

profile of v3, /device:TPU:170, one launch (start us, length us, event | category | flops | bytes accessed | tf_op | source)
XLA Modules:
  0.0 185.3 jit_solution(4403542955180705666)
XLA Ops:
  0.0 182.1 %shard_map.73 = f32[2,8,128,256]{3,2,1,0:T(8,128)} custom-call(bf16[2,64,32,8,128]{4,3,2,1,0:T(8,128)(2,1)} %bitcast.4, f32[128,256]{1,0:T(8,128)} %bitcast.5, bf16[2,8,256,256]{3,2,1,0:T(8,128)(2,1)} %w_ref.1, f32[2,16,128]{2,1,0:T(8,128)} %constant.4.clone.turn_ref, bf16[256,256]{1,0:T(8,128)(2,1)} %constant.5.clone.perm_ref, s32[4,16]{1,0:T(4,128)} %taps_ref.1, ...), custom_call_target="tpu_custom_call" | custom-call | flops 20000000000 | bytes 15000000 | tf_op jit(solution)/shard_map/pallas_call | solution.py:363
  182.1 3.1 %copy.9 = f32[2,8,8,16,256]{4,3,2,1,0:T(8,128)} copy(f32[2,8,8,16,256]{4,3,2,1,0:T(8,128)} %bitcast.3) | data formatting | bytes 4194304

commit v4 on v3

--- a/solution.py
+++ b/solution.py
@@ -25,7 +25,6 @@
 
 FRAMES = SPAN // LENGTH
 PASSED = [(0, 3), (3, 8)]
-SHIFTED = 1
 
 RUNS = [
     [(2, 1), (0, 3), (2, 3), (0, 1)],
@@ -158,9 +157,8 @@
         )
 
     def forwards(c):
-        shift = (1 - differ) * (1 - lax.div(c + 8 - SHIFTED, 8))
         return [
-            lambda: forward(c, (behind + shift * (ahead - behind)) * 2, 0, 1 - 2 * shift),
+            lambda: forward(c, behind * 2, 0, 1),
             lambda: forward(c, ahead * 2 + 1, 1, -1),
         ]
 
@@ -275,7 +273,7 @@
         )
 
     def s_copy(c):
-        return remote(ssend.at[c], sbuf.at[c, z], s_send.at[c], s_recv.at[c * 2 + z], xy * 2 + k, lax.rem(t + 1, 4) * 2)
+        return remote(ssend.at[c], sbuf.at[c, z], s_send.at[c], s_recv.at[c * 2 + z], xy * 2, lax.rem(t + 1, 4) * 2 + k)
 
     from_a = lax.rem(t + differ * (2 + z), 4)
     from_b = lax.rem(t + 2 - differ + differ * z, 4)
@@ -287,14 +285,6 @@
         for part in range(2):
             o_ref[part, c] = (obuf[c, 0, part].astype(F32) + obuf[c, 1, part].astype(F32)) * scale
 
-        @pl.when(jnp.logical_and(t > 0, k == 0))
-        def _():
-            for h in range(2):
-                arrived(sbuf.at[c, h], s_recv.at[c * 2 + h])
-            late = (sbuf[c, 0].astype(F32) + sbuf[c, 1].astype(F32)) * scale
-            for part in range(2):
-                o_ref[part, c, :SPILL] += late[part * SPILL : (part + 1) * SPILL]
-
     @pl.loop(0, 8)
     def _(c):
         for slot in (from_a * 2, from_a * 2 + 1, from_b * 2, from_b * 2 + 1):
@@ -304,19 +294,32 @@
             by_re = lax.dot_general(left, wbuf[c, :BEAMS], NT, preferred_element_type=F32)
             by_im = lax.dot_general(left, wbuf[c, BEAMS:], NT, preferred_element_type=F32)
             n = left.shape[0] // 2
-            return (by_re[:n] - by_im[n:]).astype(BF16), (by_re[n:] + by_im[:n]).astype(BF16)
-
-        ssend[c, :SPILL], ssend[c, SPILL:] = sums(spec[c, 512:ROWS])
+            return by_re[:n] - by_im[n:], by_re[n:] + by_im[:n]
+
+        for part, values in enumerate(sums(spec[c, 512:ROWS])):
+            ssend[c, part * SPILL : (part + 1) * SPILL] = values.astype(BF16)
 
         @pl.when(t < 3)
         def _():
             s_copy(c).start()
 
-        for half in range(2):
+        for half in (1, 0):
             left = jnp.concatenate(
                 [spec[c, half * 128 : half * 128 + 128], spec[c, 256 + half * 128 : 384 + half * 128]], axis=0
             )
-            osend[c, half, 0], osend[c, half, 1] = sums(left)
+            formed = sums(left)
+            for part in range(2):
+                osend[c, half, part] = formed[part].astype(BF16)
+            if half == 0:
+                @pl.when(jnp.logical_and(t > 0, z == 0))
+                def _():
+                    for h in range(2):
+                        arrived(sbuf.at[c, h], s_recv.at[c * 2 + h])
+                    for part in range(2):
+                        rows = slice(part * SPILL, (part + 1) * SPILL)
+                        late = sbuf[c, 0, rows].astype(F32) + sbuf[c, 1, rows].astype(F32)
+                        osend[c, 0, part, :SPILL] = (formed[part][:SPILL] + late).astype(BF16)
+
             here, far, near = o_copies(c, half)
             pl.when(here)(lambda near=near: near().start())
             pl.when(jnp.logical_not(here))(lambda far=far: far().start())

time: 188 us -> 184 us (0.979)
  Pallas kernels: 182 us -> 179 us
    pallas_call x1, Pallas kernels: 182 us -> 179 us  [shards(): pl.pallas_call(kernel, out_shape=jax.ShapeDtypeStruct((2, GROUP, SPAN, BE...]
where the time goes in v4:
time: 184 us; the launch traced here: 182 us
  Pallas kernels  179 us (97%)
  local copies, waits for them, and re-layouts  3.14 us (2%)
    pallas_call x1, Pallas kernels, shards(): pl.pallas_call(kernel, out_shape=jax.ShapeDtypeStruct((2, GROUP, SPAN, BE...  179 us

profile of v4, /device:TPU:170, one launch (start us, length us, event | category | flops | bytes accessed | tf_op | source)
XLA Modules:
  0.0 182.4 jit_solution(3693121041260107178)
XLA Ops:
  0.0 179.2 %shard_map.73 = f32[2,8,128,256]{3,2,1,0:T(8,128)} custom-call(bf16[2,64,32,8,128]{4,3,2,1,0:T(8,128)(2,1)} %bitcast.4, f32[128,256]{1,0:T(8,128)} %bitcast.5, bf16[2,8,256,256]{3,2,1,0:T(8,128)(2,1)} %w_ref.1, f32[2,16,128]{2,1,0:T(8,128)} %constant.4.clone.turn_ref, bf16[256,256]{1,0:T(8,128)(2,1)} %constant.5.clone.perm_ref, s32[4,16]{1,0:T(4,128)} %taps_ref.1, ...), custom_call_target="tpu_custom_call" | custom-call | flops 20000000000 | bytes 15000000 | tf_op jit(solution)/shard_map/pallas_call | solution.py:366
  179.2 3.1 %copy.9 = f32[2,8,8,16,256]{4,3,2,1,0:T(8,128)} copy(f32[2,8,8,16,256]{4,3,2,1,0:T(8,128)} %bitcast.3) | data formatting | bytes 4194304

commit v5 on v4

--- a/solution.py
+++ b/solution.py
@@ -97,6 +97,7 @@
 
     pltpu.make_async_copy(w_ref, wv, w_load).wait()
     split(0)
+    split(1)
     pl.semaphore_wait(barrier, 31 + 14)
 
     def v_copy(dx, dy, dk):
@@ -177,10 +178,11 @@
                 copy().start()
 
     send_weights(0)
+    send_weights(1)
     for dx, dy, dk in TARGETS:
         v_copy(dx, dy, dk).start()
 
-    @pl.loop(1, 8)
+    @pl.loop(2, 8)
     def _(c):
         split(c)
         send_weights(c)

time: 184 us -> 184 us (level)
  no operation moved by 1% of the time
where the time goes in v5:
time: 184 us; the launch traced here: 182 us
  Pallas kernels  179 us (97%)
  local copies, waits for them, and re-layouts  3.14 us (2%)
    pallas_call x1, Pallas kernels, shards(): pl.pallas_call(kernel, out_shape=jax.ShapeDtypeStruct((2, GROUP, SPAN, BE...  179 us

profile of v5, /device:TPU:170, one launch (start us, length us, event | category | flops | bytes accessed | tf_op | source)
XLA Modules:
  0.0 182.3 jit_solution(5959216997272918922)
XLA Ops:
  0.0 179.2 %shard_map.73 = f32[2,8,128,256]{3,2,1,0:T(8,128)} custom-call(bf16[2,64,32,8,128]{4,3,2,1,0:T(8,128)(2,1)} %bitcast.4, f32[128,256]{1,0:T(8,128)} %bitcast.5, bf16[2,8,256,256]{3,2,1,0:T(8,128)(2,1)} %w_ref.1, f32[2,16,128]{2,1,0:T(8,128)} %constant.4.clone.turn_ref, bf16[256,256]{1,0:T(8,128)(2,1)} %constant.5.clone.perm_ref, s32[4,16]{1,0:T(4,128)} %taps_ref.1, ...), custom_call_target="tpu_custom_call" | custom-call | flops 20000000000 | bytes 15000000 | tf_op jit(solution)/shard_map/pallas_call | solution.py:368
  179.2 3.1 %copy.9 = f32[2,8,8,16,256]{4,3,2,1,0:T(8,128)} copy(f32[2,8,8,16,256]{4,3,2,1,0:T(8,128)} %bitcast.3) | data formatting | bytes 4194304
